TPU v7x, 256 devices: a whole 4x4x8 slice. The times are simulated.
256 devices in a mesh: node: 4 (over x_hi, core), inner: 16 (over x_lo, z), tensor: 4 (over y).
Axes of the slice: x: 4 (x_hi: 2, x_lo: 2; x = x_hi * 2 + x_lo), y: 4, z: 8, core: 2. Of those that a mesh axis runs over, the one named last changes fastest.
Arguments:
- prev_hidden: bfloat16 [8192, 14336], P(('node', 'inner'), 'tensor'), may hold values from -6 to 6
- prev_cot: bfloat16 [8192, 4096], P(('node', 'inner')), may hold values from -16 to 16
- next_hidden: bfloat16 [8192, 14336], P(('node', 'inner'), 'tensor'), may hold values from -6 to 6
- weight: float32 [4096, 14336], P(('node', 'inner'), 'tensor'), may hold values from -0.3 to 0.3
- moment1: float32 [4096, 14336], P(('node', 'inner'), 'tensor'), may hold values from -0.03314563 to 0.03314563
- moment2: float32 [4096, 14336], P(('node', 'inner'), 'tensor'), may hold values from 1.2207031e-05 to 0.0012207031
Outputs:
- ffn_out: bfloat16 [8192, 4096], P(('node', 'inner'), 'tensor')
- new_weight: float32 [4096, 14336], P(('node', 'inner'), 'tensor')
- new_moment1: float32 [4096, 14336], P(('node', 'inner'), 'tensor')
- new_moment2: float32 [4096, 14336], P(('node', 'inner'), 'tensor')
All inputs are finite; a program needn't handle non-finite values.
Results may differ from a plain program's by a relative error of at most 0.013.
Values may be sent and summed in bfloat16 or wider, within the bound.
A program may use at most 256 MiB of HBM per device.

v0:
```python
import math

import jax
import jax.numpy as jnp
from jax import lax
from jax.sharding import PartitionSpec as P

FB = 14336
ADAM_STEP = 20


def term_rows(cotangent, hidden):
    return lax.dot_general(
        cotangent, hidden, (((0,), (0,)), ((), ())), preferred_element_type=jnp.float32
    )


def on_device(prev_hidden, prev_cot, next_hidden, weight, moment1, moment2):
    tok_rows = prev_cot.shape[0]
    node_count = lax.axis_size("node")
    inner_count = lax.axis_size("inner")
    all_tokens = tok_rows * node_count * inner_count
    factor = 1.0 / math.sqrt(FB)
    summed = lax.psum_scatter(
        term_rows(prev_cot, prev_hidden), ("node", "inner"), scatter_dimension=0, tiled=True
    )
    gradient = summed / all_tokens
    new_moment1 = 0.9 * moment1 + 0.1 * gradient
    new_moment2 = 0.95 * moment2 + 0.05 * gradient * gradient
    first_fix = 1.0 - 0.9**ADAM_STEP
    second_fix = 1.0 - 0.95**ADAM_STEP
    ratio = new_moment1 / first_fix / (jnp.sqrt(new_moment2 / second_fix) + 1e-08)
    new_weight = weight - 0.05 * (ratio + 0.1 * weight)
    weight_copy = new_weight.astype(jnp.bfloat16)
    secondary = lax.all_gather(weight_copy[None], "node", axis=0, tiled=True)
    outputs = jnp.einsum(
        "tf,nkf->tnk",
        next_hidden,
        lax.all_gather(secondary, "inner", axis=1, tiled=True),
        preferred_element_type=jnp.float32,
    )
    scaled = outputs.reshape(tok_rows, -1) * factor
    ffn_out = lax.psum_scatter(
        scaled.astype(jnp.bfloat16), "tensor", scatter_dimension=1, tiled=True
    )
    return (ffn_out, new_weight, new_moment1, new_moment2)


def solution(mesh):
    in_specs = (
        P(("node", "inner"), "tensor"),
        P(("node", "inner"), None),
        P(("node", "inner"), "tensor"),
        P(("node", "inner"), "tensor"),
        P(("node", "inner"), "tensor"),
        P(("node", "inner"), "tensor"),
    )
    out_specs = (
        P(("node", "inner"), "tensor"),
        P(("node", "inner"), "tensor"),
        P(("node", "inner"), "tensor"),
        P(("node", "inner"), "tensor"),
    )
    return jax.shard_map(
        on_device, mesh=mesh, in_specs=in_specs, out_specs=out_specs, check_vma=False
    )
```

profile of v0, /device:TPU:1, one launch (start us, length us, event | category | flops | bytes accessed | tf_op | source)
XLA Modules:
  0.0 1058.8 jit_solution(12925516745829613926)
XLA Ops:
  7.2 0.0 copy-start
  7.2 0.0 reduce-scatter.3.cloned.1.call-start
  7.2 1.2 copy-done
  8.4 23.7 %fusion.2 = f32[4096,3584]{1,0:T(8,128)} fusion(bf16[128,4096]{1,0:T(8,128)(2,1)S(1)} %copy-done, bf16[128,3584]{1,0:T(8,128)(2,1)} %param.6), kind=kOutput, calls=%fused_computation.6 | convolution fusion | flops 3758096384 | bytes 60686336 | tf_op jit(solution)/shard_map/dot_general | solution.py:13
  32.1 0.0 copy-start.2
  32.1 0.0 copy-start.3
  32.1 0.0 reduce-scatter.3.cloned.1.call-update
  32.1 0.0 copy-start.1
  32.1 0.0 all-gather.6.cloned.1.call-start
  32.2 640.6 %reduce-scatter.3.cloned.1.call-done = f32[64,3584]{1,0:T(8,128)} async-done(((f32[4096,3584]{1,0:T(8,128)}), f32[64,3584]{1,0:T(8,128)}) %reduce-scatter.3.cloned.1.call-update) | async-done | bytes 917520 | tf_op jit(solution)/shard_map/reduce_scatter | solution.py:24
  672.8 0.0 copy-done.2
  672.8 0.0 copy-done.3
  672.8 3.6 fusion.1
  676.4 0.0 all-gather.6.cloned.1.call-update
  676.4 0.0 all-gather.4.cloned.1.call-start
  676.5 25.7 %all-gather.6.cloned.1.call-done = bf16[256,3584]{1,0:T(8,128)(2,1)} async-done(((bf16[64,3584]{1,0:T(8,128)(2,1)}), bf16[256,3584]{1,0:T(8,128)(2,1)}) %all-gather.6.cloned.1.call-update) | async-done | bytes 1835024 | tf_op jit(solution)/shard_map/all_gather | solution.py:35
  702.2 0.0 all-gather.4.cloned.1.call-update
  702.2 0.0 reduce-scatter.5.cloned.1.call-start
  702.2 312.5 %all-gather.4.cloned.1.call-done = bf16[4,1024,3584]{2,1,0:T(8,128)(2,1)} async-done(((bf16[4,64,3584]{2,1,0:T(8,128)(2,1)}), bf16[4,1024,3584]{2,1,0:T(8,128)(2,1)}) %all-gather.4.cloned.1.call-update) | async-done | bytes 29360144 | tf_op jit(solution)/shard_map/all_gather | solution.py:39
  1014.7 13.6 %multiply_convert_fusion = bf16[4,1024,128]{2,1,0:T(8,128)(2,1)S(1)} fusion(bf16[4,1024,3584]{2,1,0:T(8,128)(2,1)} %all-gather.4.cloned.1.call-done, bf16[128,3584]{1,0:T(8,128)(2,1)} %param.8), kind=kOutput, calls=%fused_computation | convolution fusion | flops 3759144960 | bytes 31326208 | tf_op jit(solution)/shard_map/tf,nkf->tnk/dot_general | solution.py:36
  1028.3 1.3 copy.10
  1029.6 0.0 reduce-scatter.5.cloned.1.call-update
  1029.6 22.6 %reduce-scatter.5.cloned.1.call-done = bf16[128,1024]{1,0:T(8,128)(2,1)} async-done(((bf16[128,4096]{1,0:T(8,128)(2,1)}), bf16[128,1024]{1,0:T(8,128)(2,1)}) %reduce-scatter.5.cloned.1.call-update) | async-done | bytes 262160 | tf_op jit(solution)/shard_map/reduce_scatter | solution.py:43
  1052.2 0.0 copy-done.1
Async XLA Ops:
  7.2 1.2 copy-start
  7.2 665.6 %reduce-scatter.3.cloned.1.call-start = ((), (), s32[]{:S(2)}) async-start(), calls=%async_computation.2 | async-start | bytes 59637760 | tf_op jit(solution)/shard_map/reduce_scatter | solution.py:24
  32.1 640.7 %copy-start.2 = (f32[64,3584]{1,0:T(8,128)S(1)}, f32[64,3584]{1,0:T(8,128)}, u32[]{:S(2)}) copy-start(f32[64,3584]{1,0:T(8,128)} %param.9) | copy-start | bytes 2752516
  32.1 640.7 %copy-start.3 = (f32[64,3584]{1,0:T(8,128)S(1)}, f32[64,3584]{1,0:T(8,128)}, u32[]{:S(2)}) copy-start(f32[64,3584]{1,0:T(8,128)} %param.10) | copy-start | bytes 2752516
  32.1 1020.1 %copy-start.1 = (bf16[128,4096]{1,0:T(8,128)(2,1)S(1)}, bf16[128,4096]{1,0:T(8,128)(2,1)}, u32[]{:S(2)}) copy-start(bf16[128,4096]{1,0:T(8,128)(2,1)} %param.7) | copy-start | bytes 3145732
  32.1 670.0 %all-gather.6.cloned.1.call-start = ((), (), s32[]{:S(2)}) async-start(), calls=%async_computation.5 | async-start | bytes 2293760 | tf_op jit(solution)/shard_map/all_gather | solution.py:35
  676.4 338.2 %all-gather.4.cloned.1.call-start = ((), (), s32[]{:S(2)}) async-start(), calls=%async_computation.3 | async-start | bytes 31195136 | tf_op jit(solution)/shard_map/all_gather | solution.py:39
  702.2 350.0 %reduce-scatter.5.cloned.1.call-start = ((), (), s32[]{:S(2)}) async-start(), calls=%async_computation.4 | async-start | bytes 1310720 | tf_op jit(solution)/shard_map/reduce_scatter | solution.py:43
Sparse Core Ops, SparseCore 0:
  32.2 640.5 reduce-scatter.2
  676.6 25.5 all-gather.5
  704.0 310.6 all-gather.3
  1029.8 22.4 reduce-scatter.4
where the time goes:
time: 1060 us
  waiting for transfers between devices  1000 us (94%)
  matrix products  37.3 us (4%)
  between operations  13.8 us (1%)
    reduce_scatter x1, waiting for transfers between devices, on_device(): lax.psum_scatter(term_rows(prev_cot, prev_hidden), ('node', 'inner'), sca...  641 us
    all_gather x1, waiting for transfers between devices, on_device(): lax.all_gather(secondary, 'inner', axis=1, tiled=True)  312 us
    all_gather x1, waiting for transfers between devices, on_device(): secondary = lax.all_gather(weight_copy[None], 'node', axis=0, tiled=True)  25.7 us
    dot_general x1, matrix products, term_rows(): lax.dot_general(cotangent, hidden, (((0,), (0,)), ((), ())), preferred_el...  23.7 us
    reduce_scatter x1, waiting for transfers between devices, on_device(): lax.psum_scatter(scaled.astype(jnp.bfloat16), 'tensor', scatter_dimension...  22.6 us
  transfers between devices with their start and end apart: 4, of which 4 were waited for; matrix products, arithmetic and copies ran while one was open for 0% of the time, Pallas kernels for 0%

commit v1 on v0

v1 whole, which is shorter than its diff:
```python
import functools
import math

import jax
import jax.numpy as jnp
from jax import lax
from jax.experimental import pallas as pl
from jax.experimental.pallas import tpu as pltpu
from jax.sharding import PartitionSpec as P

FB = 14336
ADAM_STEP = 20
MESH = pl.DeviceIdType.MESH
XS = 4
CUT = 512
LAG_X = 1
LAG_Z = 1
NEXT_AT = 4


def kernel(
    zs, cut, lag_x, lag_z, next_at,
    hid_ref, cot_ref, nxt_ref, w_ref, m1_ref, m2_ref,
    ffn_ref, nw_ref, nm1_ref, nm2_ref,
    hbuf, xbuf, cbuf, ct, grad, send_p, send_m, recv_p, recv_m, wv, m1v, m2v, wall, acc, part, got, fin,
    x_send, x_recv, x_own, c_send, c_recv, c_own, rs_send, rs_recv, ag_send, ag_recv,
    o_send, o_recv, loads, stores, last,
):
    tok, cols = hid_ref.shape
    rows = w_ref.shape[0]
    n = cols // cut
    steps = zs // 2
    feats = rows * zs
    all_tokens = tok * zs * XS * 2 * 1
    factor = 1.0 / math.sqrt(FB)

    node, inner, ten = lax.axis_index("node"), lax.axis_index("inner"), lax.axis_index("tensor")
    core, x_lo, z = lax.rem(node, 2), lax.div(inner, zs), lax.rem(inner, zs)
    x = lax.div(node, 2) * 2 + x_lo

    def at(px, pz, pc, py):
        return (lax.div(px, 2) * 2 + pc, lax.rem(px, 2) * zs + pz, py)

    def row_peer(j, dc):
        return lax.rem(x + j, XS), lax.rem(core + dc, 2)

    def row_device(j, dc):
        px, pc = row_peer(j, dc)
        return at(px, z, pc, ten)

    def z_device(d):
        return at(x, lax.rem(z + d + zs, zs), core, ten)

    barrier = pltpu.get_barrier_semaphore()
    at_home = node == ten
    for j in range(XS):
        for dc in range(2):
            if j or dc:
                pl.semaphore_signal(barrier, inc=1, device_id=row_device(j, dc), device_id_type=MESH)
    for d in (1, -1):
        pl.semaphore_signal(barrier, inc=1, device_id=z_device(d), device_id_type=MESH)
    for lo in range(2):
        for py in range(4):
            mine = at_home & (x_lo == lo) & (ten == py)

            @pl.when(jnp.logical_not(mine))
            def _():
                pl.semaphore_signal(
                    barrier, inc=1, device_id=(ten, lo * zs + z, jnp.int32(py)), device_id_type=MESH
                )

    load_w = pltpu.make_async_copy(w_ref, wv, loads.at[0])
    load_m1 = pltpu.make_async_copy(m1_ref, m1v, loads.at[1])
    load_m2 = pltpu.make_async_copy(m2_ref, m2v, loads.at[2])

    def block_of(px, pc):
        return (lax.div(px, 2) * 2 + pc) * 2 + lax.rem(px, 2)

    def cot_columns(px, pc):
        return cot_ref.at[:, pl.ds(pl.multiple_of(block_of(px, pc) * feats, feats), feats)]

    own_c = pltpu.make_async_copy(cot_columns(x, core), cbuf.at[0], c_own)

    def c_copy(j, dc):
        px, pc = row_peer(j, dc)
        slot = ((XS - j) % XS) * 2 + dc
        return pltpu.make_async_remote_copy(
            src_ref=cot_columns(px, pc), dst_ref=cbuf.at[slot], send_sem=c_send.at[slot],
            recv_sem=c_recv.at[slot], device_id=at(px, z, pc, ten), device_id_type=MESH,
        )

    def chunk(k):
        return pl.ds(pl.multiple_of(k * cut, cut), cut)

    def x_own_copy(a, k):
        ref, buf = (hid_ref, hbuf) if a == 0 else (nxt_ref, xbuf)
        return pltpu.make_async_copy(ref.at[:, chunk(k)], buf.at[k, 0], x_own.at[a, k])

    def x_copy(a, k, i):
        ref, buf = (hid_ref, hbuf) if a == 0 else (nxt_ref, xbuf)
        half = tok // 2
        first, second = pl.ds(0, half), pl.ds(half, half)
        src, dst, peer = {
            0: (ref.at[:, chunk(k)], buf.at[k, 1], (0, 1)),
            1: (ref.at[:, chunk(k)], buf.at[k, 2], (XS - 1, 0)),
            2: (ref.at[:, chunk(k)], buf.at[k, 6], (1, 0)),
            3: (buf.at[k, 6, first], buf.at[k, 4, first], (1, 0)),
            4: (buf.at[k, 2, second], buf.at[k, 4, second], (XS - 1, 0)),
            5: (buf.at[k, 2], buf.at[k, 3], (0, 1)),
            6: (buf.at[k, 6], buf.at[k, 7], (0, 1)),
            7: (buf.at[k, 4], buf.at[k, 5], (0, 1)),
        }[i]
        return pltpu.make_async_remote_copy(
            src_ref=src, dst_ref=dst, send_sem=x_send.at[a, k, i], recv_sem=x_recv.at[a, k, i],
            device_id=row_device(*peer), device_id_type=MESH,
        )

    half_rows = rows // 2
    part_of = (pl.ds(0, half_rows), pl.ds(half_rows, half_rows))

    def rs_copy(k, d, s):
        src, dst = (send_p, recv_p) if d == 0 else (send_m, recv_m)
        src, dst = src.at[k, s], dst.at[k, s]
        if s == 0:
            src, dst = src.at[part_of[d]], dst.at[part_of[d]]
        return pltpu.make_async_remote_copy(
            src_ref=src, dst_ref=dst, send_sem=rs_send.at[k, d, s], recv_sem=rs_recv.at[k, d, s],
            device_id=z_device(1 - 2 * d), device_id_type=MESH,
        )

    def ag_copy(k, d, s, arriving=False):
        far = s + 1 if arriving else s
        slot = lax.rem(z + (zs - far if d == 0 else far), zs)
        ref = wall.at[k, slot]
        if s == steps - 1:
            ref = ref.at[part_of[d]]
        return pltpu.make_async_remote_copy(
            src_ref=ref, dst_ref=ref, send_sem=ag_send.at[k, d, s], recv_sem=ag_recv.at[k, d, s],
            device_id=z_device(1 - 2 * d), device_id_type=MESH,
        )

    def store(k, i):
        src, dst = ((wv, nw_ref), (m1v, nm1_ref), (m2v, nm2_ref))[i]
        return pltpu.make_async_copy(src.at[:, chunk(k)], dst.at[:, chunk(k)], stores.at[i, k])

    own_c.start()
    load_w.start()
    load_m1.start()
    load_m2.start()
    pl.semaphore_wait(barrier, 7 + 2 + 8 - jnp.where(at_home, 1, 0))
    for j in (2, 1, 3, 0):
        for dc in (0, 1):
            if j or dc:
                c_copy(j, dc).start()
    acc[...] = jnp.zeros_like(acc)

    def x_first(a, k):
        x_own_copy(a, k).start()
        for i in (1, 2, 0):
            x_copy(a, k, i).start()

    def x_second(a, k):
        x_copy(a, k, 2).wait_recv()
        x_copy(a, k, 3).start()
        x_copy(a, k, 1).wait_recv()
        x_copy(a, k, 4).start()
        x_copy(a, k, 5).start()
        x_copy(a, k, 6).start()

    def x_third(a, k):
        x_copy(a, k, 3).wait_recv()
        x_copy(a, k, 4).wait_recv()
        x_copy(a, k, 7).start()

    def x_done(a, k):
        x_own_copy(a, k).wait()
        for i in (0, 5, 6, 7):
            x_copy(a, k, i).wait_recv()

    def multiply(k):
        @pl.when(k == 0)
        def _():
            own_c.wait()
            for j in range(XS):
                for dc in range(2):
                    if j or dc:
                        c_copy(j, dc).wait_recv()
            for slot in range(2 * XS):
                ct[:, slot * tok:(slot + 1) * tok] = cbuf[slot].T

        x_done(0, k)
        block = hbuf[k].reshape(2 * XS * tok, cut)
        tile = min(4, zs)
        for i in range(zs // tile):
            sums = jnp.dot(
                ct[i * tile * rows:(i + 1) * tile * rows, :], block, preferred_element_type=jnp.float32
            )
            grad[k, i * tile:(i + 1) * tile] = sums.reshape(tile, rows, cut)
        opposite = grad[k, lax.rem(z + steps, zs)].astype(jnp.bfloat16)
        send_p[k, 0] = opposite
        send_m[k, 0] = opposite
        rs_copy(k, 0, 0).start()
        rs_copy(k, 1, 0).start()

    def rs_step(k, s):
        for d in range(2):
            src, dst = (send_p, recv_p) if d == 0 else (send_m, recv_m)
            rs_copy(k, d, s - 1).wait_recv()
            far = steps - s
            own = grad.at[k, lax.rem(z + (far if d == 0 else zs - far), zs)]
            if s == 1:
                with_it, without = (0, half_rows) if d == 0 else (half_rows, 0)
                a, b = pl.ds(with_it, half_rows), pl.ds(without, half_rows)
                src[k, s, a] = (own[a] + dst[k, 0, a].astype(jnp.float32)).astype(jnp.bfloat16)
                src[k, s, b] = own[b].astype(jnp.bfloat16)
            else:
                src[k, s] = (own[...] + dst[k, s - 1].astype(jnp.float32)).astype(jnp.bfloat16)
            rs_copy(k, d, s).start()

    def adam(k):
        @pl.when(k == 0)
        def _():
            load_w.wait()
            load_m1.wait()
            load_m2.wait()

        rs_copy(k, 0, steps - 1).wait_recv()
        rs_copy(k, 1, steps - 1).wait_recv()
        summed = (
            grad[k, z]
            + recv_p[k, steps - 1].astype(jnp.float32)
            + recv_m[k, steps - 1].astype(jnp.float32)
        )
        gradient = summed / all_tokens
        here = chunk(k)
        new_moment1 = 0.9 * m1v[:, here] + 0.1 * gradient
        new_moment2 = 0.95 * m2v[:, here] + 0.05 * gradient * gradient
        first_fix = 1.0 - 0.9**ADAM_STEP
        second_fix = 1.0 - 0.95**ADAM_STEP
        ratio = new_moment1 / first_fix / (jnp.sqrt(new_moment2 / second_fix) + 1e-08)
        weight = wv[:, here]
        new_weight = weight - 0.05 * (ratio + 0.1 * weight)
        wall[k, z] = new_weight.astype(jnp.bfloat16)
        ag_copy(k, 0, 0).start()
        ag_copy(k, 1, 0).start()
        wv[:, here] = new_weight
        m1v[:, here] = new_moment1
        m2v[:, here] = new_moment2
        for i in range(3):
            store(k, i).start()

    def ag_step(k, s):
        for d in range(2):
            ag_copy(k, d, s - 1, arriving=True).wait_recv()
            ag_copy(k, d, s).start()

    def forward(k):
        for d in range(2):
            ag_copy(k, d, steps - 1, arriving=True).wait_recv()
        x_done(1, k)
        copy = wall[k].reshape(feats, cut)
        for i in range(XS):
            block = xbuf[k, 2 * i:2 * i + 2].reshape(2 * tok, cut)
            acc[2 * i * tok:2 * (i + 1) * tok, :] += lax.dot_general(
                block, copy, (((1,), (1,)), ((), ())), preferred_element_type=jnp.float32
            )

    at_mul = 3 * lag_x
    at_adam = at_mul + steps * lag_z
    at_out = max(at_adam + steps * lag_z, next_at + 3 * lag_x)
    plan = []
    for s in range(steps - 1, 0, -1):
        plan.append((at_adam + s * lag_z, functools.partial(ag_step, s=s)))
    for s in range(steps - 1, 0, -1):
        plan.append((at_mul + s * lag_z, functools.partial(rs_step, s=s)))
    plan.append((at_adam, adam))
    for a, base in ((0, 0), (1, next_at)):
        plan.append((base + 2 * lag_x, functools.partial(x_third, a)))
        plan.append((base + lag_x, functools.partial(x_second, a)))
        plan.append((base, functools.partial(x_first, a)))
    plan.append((at_mul, multiply))
    plan.append((at_out, forward))

    def tick(t, carry):
        for start, stage in plan:
            k = t - start

            @pl.when((k >= 0) & (k < n))
            def _(k=k, stage=stage):
                stage(k)

        return carry

    lax.fori_loop(0, at_out + n, tick, 0)

    def o_copy(j, dc):
        px, pc = row_peer(j, dc)
        return pltpu.make_async_remote_copy(
            src_ref=part.at[2 * j + dc], dst_ref=got.at[ten * 2 + x_lo], send_sem=o_send.at[2 * j + dc],
            recv_sem=o_recv.at[ten * 2 + x_lo], device_id=at(px, z, pc, node), device_id_type=MESH,
        )

    stay = pltpu.make_async_copy(part.at[0], got.at[ten * 2 + x_lo], o_recv.at[ten * 2 + x_lo])
    for j in (2, 1, 3, 0):
        for dc in range(2):
            slot = 2 * j + dc
            part[slot] = (acc[slot * tok:(slot + 1) * tok, :] * factor).astype(jnp.bfloat16)
            if slot:
                o_copy(j, dc).start()
            else:

                @pl.when(at_home)
                def _():
                    stay.start()

                @pl.when(jnp.logical_not(at_home))
                def _():
                    o_copy(0, 0).start()

    for j in range(XS):
        for dc in range(2):
            if j or dc:
                c_copy(j, dc).wait_send()

    def drain(k, carry):
        for a in range(2):
            for i in range(8):
                x_copy(a, k, i).wait_send()
        for d in range(2):
            for s in range(steps):
                rs_copy(k, d, s).wait_send()
                ag_copy(k, d, s).wait_send()
        for i in range(3):
            store(k, i).wait()
        return carry

    lax.fori_loop(0, n, drain, 0)

    for lo in range(2):
        total = jnp.zeros((tok, feats), jnp.float32)
        for py in range(4):
            slot = 2 * py + lo
            pltpu.make_async_copy(part.at[0], got.at[slot], o_recv.at[slot]).wait()
            total = total + got[slot].astype(jnp.float32)
        fin[:, lo * feats:(lo + 1) * feats] = total.astype(jnp.bfloat16)
    out = pltpu.make_async_copy(fin, ffn_ref, last)
    out.start()
    for j in range(XS):
        for dc in range(2):
            if j or dc:
                o_copy(j, dc).wait_send()

    @pl.when(jnp.logical_not(at_home))
    def _():
        o_copy(0, 0).wait_send()

    out.wait()


def on_device(prev_hidden, prev_cot, next_hidden, weight, moment1, moment2):
    tok, cols = prev_hidden.shape
    rows, features = weight.shape[0], prev_cot.shape[1]
    zs = lax.axis_size("inner") // 2
    steps = zs // 2
    cut = min(CUT, cols // 2)
    n = cols // cut
    feats = rows * zs
    bf16, f32 = jnp.bfloat16, jnp.float32
    dma = pltpu.SemaphoreType.DMA
    anywhere = pl.BlockSpec(memory_space=pl.ANY)
    return pl.pallas_call(
        functools.partial(kernel, zs, cut, LAG_X, LAG_Z, NEXT_AT),
        out_shape=(
            jax.ShapeDtypeStruct((tok, features // 4), bf16),
            jax.ShapeDtypeStruct(weight.shape, f32),
            jax.ShapeDtypeStruct(weight.shape, f32),
            jax.ShapeDtypeStruct(weight.shape, f32),
        ),
        in_specs=[anywhere] * 6,
        out_specs=(anywhere,) * 4,
        scratch_shapes=[
            pltpu.VMEM((n, 2 * XS, tok, cut), bf16),
            pltpu.VMEM((n, 2 * XS, tok, cut), bf16),
            pltpu.VMEM((2 * XS, tok, feats), bf16),
            pltpu.VMEM((feats, 2 * XS * tok), bf16),
            pltpu.VMEM((n, zs, rows, cut), f32),
            pltpu.VMEM((n, steps, rows, cut), bf16),
            pltpu.VMEM((n, steps, rows, cut), bf16),
            pltpu.VMEM((n, steps, rows, cut), bf16),
            pltpu.VMEM((n, steps, rows, cut), bf16),
            pltpu.VMEM((rows, cols), f32),
            pltpu.VMEM((rows, cols), f32),
            pltpu.VMEM((rows, cols), f32),
            pltpu.VMEM((n, zs, rows, cut), bf16),
            pltpu.VMEM((2 * XS * tok, feats), f32),
            pltpu.VMEM((2 * XS, tok, feats), bf16),
            pltpu.VMEM((2 * XS, tok, feats), bf16),
            pltpu.VMEM((tok, 2 * feats), bf16),
            dma((2, n, 8)),
            dma((2, n, 8)),
            dma((2, n)),
            dma((2 * XS,)),
            dma((2 * XS,)),
            dma(()),
            dma((n, 2, steps)),
            dma((n, 2, steps)),
            dma((n, 2, steps)),
            dma((n, 2, steps)),
            dma((2 * XS,)),
            dma((2 * XS,)),
            dma((3,)),
            dma((3, n)),
            dma(()),
        ],
        compiler_params=pltpu.CompilerParams(
            collective_id=0, has_side_effects=True, vmem_limit_bytes=56 * 2**20
        ),
    )(prev_hidden, prev_cot, next_hidden, weight, moment1, moment2)


def solution(mesh):
    split = P(("node", "inner"), "tensor")
    return jax.shard_map(
        on_device,
        mesh=mesh,
        in_specs=(split, P(("node", "inner"), None), split, split, split, split),
        out_specs=(split,) * 4,
        check_vma=False,
    )
```

time: 1060 us -> 158 us (0.15)
  waiting for transfers between devices: 1000 us -> 0 us
  Pallas kernels: 0 us -> 150 us
  matrix products: 37.3 us -> 0 us
  between operations: 13.8 us -> 0.64 us
    reduce_scatter x2 -> x0, waiting for transfers between devices: 663 us -> none  [the longest x1 641 us: on_device(): lax.psum_scatter(term_rows(prev_cot, prev_hidden), ('node', 'inner'), sca...]
    all_gather x2 -> x0, waiting for transfers between devices: 338 us -> none  [the longest x1 312 us: on_device(): lax.all_gather(secondary, 'inner', axis=1, tiled=True)]
    pallas_call x0 -> x1, Pallas kernels: none -> 150 us  [on_device(): pl.pallas_call(functools.partial(kernel, zs, cut, LAG_X, LAG_Z, NEXT_AT),...]
    dot_general x2 -> x0, matrix products: 37.3 us -> none  [the longest x1 23.7 us: term_rows(): lax.dot_general(cotangent, hidden, (((0,), (0,)), ((), ())), preferred_el...]
  transfers between devices with their start and end apart: 4 -> 0, of which waited for: 4 -> 0; matrix products, arithmetic and copies ran while one was open for 0% -> 0% of each run, Pallas kernels for 0% -> 0%
where the time goes in v1:
time: 158 us; the launch traced here: 157 us
  Pallas kernels  150 us (95%)
  local copies, waits for them, and re-layouts  6.35 us (4%)
    pallas_call x1, Pallas kernels, on_device(): pl.pallas_call(functools.partial(kernel, zs, cut, LAG_X, LAG_Z, NEXT_AT),...  150 us
    unnamed x8, local copies, waits for them, and re-layouts  6.35 us

profile of v1, /device:TPU:1, one launch (start us, length us, event | category | flops | bytes accessed | tf_op | source)
XLA Modules:
  0.0 157.5 jit_solution(12730587988647272228)
XLA Ops:
  0.6 150.5 %shard_map.93 = (bf16[128,1024]{1,0:T(8,128)(2,1)}, f32[64,3584]{1,0:T(8,128)}, f32[64,3584]{1,0:T(8,128)}, f32[64,3584]{1,0:T(8,128)}) custom-call(bf16[128,3584]{1,0:T(8,128)(2,1)} %hid_ref.1, bf16[128,4096]{1,0:T(8,128)(2,1)} %cot_ref.1, bf16[128,3584]{1,0:T(8,128)(2,1)} %nxt_ref.1, f32[64,3584]{1,0:T(8,128)} %w_ref.1, f32[64,3584]{1,0:T(8,128)} %m1_ref.1, ...), custom_call_target="tpu_custom_call" | custom-call | tf_op jit(solution)/shard_map/pallas_call | solution.py:371
  151.1 1.7 %copy.14 = bf16[128,1024]{1,0:T(8,128)(2,1)} copy(bf16[128,1024]{1,0:T(8,128)(2,1)} %get-tuple-element.8) | data formatting | bytes 524288
  152.8 0.0 copy-start.1
  152.8 2.2 %copy.15 = f32[64,3584]{1,0:T(8,128)} copy(f32[64,3584]{1,0:T(8,128)} %get-tuple-element.9) | data formatting | bytes 1835008
  155.0 0.0 copy-done.1
  155.0 0.0 copy-start
  155.0 0.9 copy.16
  156.0 0.6 copy-done
  156.5 0.9 copy.17
Async XLA Ops:
  152.8 2.3 %copy-start.1 = (f32[64,3584]{1,0:T(8,128)S(1)}, f32[64,3584]{1,0:T(8,128)}, u32[]{:S(2)}) copy-start(f32[64,3584]{1,0:T(8,128)} %get-tuple-element.10) | copy-start | bytes 2752516
  155.0 1.5 copy-start

commit v2 on v1

--- a/solution.py
+++ b/solution.py
@@ -12,18 +12,18 @@
 ADAM_STEP = 20
 MESH = pl.DeviceIdType.MESH
 XS = 4
-CUT = 512
-LAG_X = 1
-LAG_Z = 1
-NEXT_AT = 4
+CUT = 256
+ORDER = ["C", "Y2", "X3", "Y3", "Y1", "X2", "G1", "G3", "R1", "A", "R3", "X1", "M", "O", "G2", "R2"]
+DELAY = [3, 22, 6, 29, 16, 4, 21, 31, 8, 17, 11, 1, 6, 35, 25, 9]
+SIDE = (0, 1, XS - 1, 2)
 
 
 def kernel(
-    zs, cut, lag_x, lag_z, next_at,
+    zs, cut, order, delay,
     hid_ref, cot_ref, nxt_ref, w_ref, m1_ref, m2_ref,
     ffn_ref, nw_ref, nm1_ref, nm2_ref,
     hbuf, xbuf, cbuf, ct, grad, send_p, send_m, recv_p, recv_m, wv, m1v, m2v, wall, acc, part, got, fin,
-    x_send, x_recv, x_own, c_send, c_recv, c_own, rs_send, rs_recv, ag_send, ag_recv,
+    x_send, x_recv, x_own, c_send, c_recv, c_own, y_send, y_recv, rs_send, rs_recv, ag_send, ag_recv,
     o_send, o_recv, loads, stores, last,
 ):
     tok, cols = hid_ref.shape
@@ -31,7 +31,7 @@
     n = cols // cut
     steps = zs // 2
     feats = rows * zs
-    all_tokens = tok * zs * XS * 2 * 1
+    all_tokens = tok * zs * XS * 2
     factor = 1.0 / math.sqrt(FB)
 
     node, inner, ten = lax.axis_index("node"), lax.axis_index("inner"), lax.axis_index("tensor")
@@ -50,6 +50,9 @@
 
     def z_device(d):
         return at(x, lax.rem(z + d + zs, zs), core, ten)
+
+    def y_device(d):
+        return at(x, z, core, lax.rem(ten + d + 4, 4))
 
     barrier = pltpu.get_barrier_semaphore()
     at_home = node == ten
@@ -59,6 +62,7 @@
                 pl.semaphore_signal(barrier, inc=1, device_id=row_device(j, dc), device_id_type=MESH)
     for d in (1, -1):
         pl.semaphore_signal(barrier, inc=1, device_id=z_device(d), device_id_type=MESH)
+        pl.semaphore_signal(barrier, inc=1, device_id=y_device(d), device_id_type=MESH)
     for lo in range(2):
         for py in range(4):
             mine = at_home & (x_lo == lo) & (ten == py)
@@ -76,17 +80,30 @@
     def block_of(px, pc):
         return (lax.div(px, 2) * 2 + pc) * 2 + lax.rem(px, 2)
 
-    def cot_columns(px, pc):
-        return cot_ref.at[:, pl.ds(pl.multiple_of(block_of(px, pc) * feats, feats), feats)]
-
-    own_c = pltpu.make_async_copy(cot_columns(x, core), cbuf.at[0], c_own)
-
-    def c_copy(j, dc):
-        px, pc = row_peer(j, dc)
-        slot = ((XS - j) % XS) * 2 + dc
-        return pltpu.make_async_remote_copy(
-            src_ref=cot_columns(px, pc), dst_ref=cbuf.at[slot], send_sem=c_send.at[slot],
-            recv_sem=c_recv.at[slot], device_id=at(px, z, pc, ten), device_id_type=MESH,
+    def cot_block(px, pc):
+        return pl.ds(pl.multiple_of(block_of(px, pc) * feats, feats), feats)
+
+    half, quarter = tok // 2, tok // 4
+    parity = lax.rem(ten, 2)
+    here_rows = pl.multiple_of(parity * half, half)
+    there_rows = pl.multiple_of((1 - parity) * half, half)
+    own_c = pltpu.make_async_copy(cot_ref.at[:, cot_block(x, core)], cbuf.at[0], c_own)
+
+    def c_copy(i, dc):
+        px, pc = row_peer(SIDE[i], dc)
+        slot = 2 * (0, 2, 1, 3)[i] + dc
+        part_rows = pl.ds(here_rows, half) if i else pl.ds(0, tok)
+        return pltpu.make_async_remote_copy(
+            src_ref=cot_ref.at[part_rows, cot_block(px, pc)], dst_ref=cbuf.at[slot, part_rows],
+            send_sem=c_send.at[slot], recv_sem=c_recv.at[slot], device_id=at(px, z, pc, ten), device_id_type=MESH,
+        )
+
+    def y_copy(d, arriving=False):
+        first = there_rows if arriving else here_rows
+        ref = cbuf.at[2:2 * XS, pl.ds(pl.multiple_of(first + d * quarter, quarter), quarter)]
+        return pltpu.make_async_remote_copy(
+            src_ref=ref, dst_ref=ref, send_sem=y_send.at[d], recv_sem=y_recv.at[d],
+            device_id=y_device(1 - 2 * d), device_id_type=MESH,
         )
 
     def chunk(k):
@@ -98,20 +115,16 @@
 
     def x_copy(a, k, i):
         ref, buf = (hid_ref, hbuf) if a == 0 else (nxt_ref, xbuf)
-        half = tok // 2
         first, second = pl.ds(0, half), pl.ds(half, half)
         src, dst, peer = {
-            0: (ref.at[:, chunk(k)], buf.at[k, 1], (0, 1)),
-            1: (ref.at[:, chunk(k)], buf.at[k, 2], (XS - 1, 0)),
-            2: (ref.at[:, chunk(k)], buf.at[k, 6], (1, 0)),
-            3: (buf.at[k, 6, first], buf.at[k, 4, first], (1, 0)),
-            4: (buf.at[k, 2, second], buf.at[k, 4, second], (XS - 1, 0)),
-            5: (buf.at[k, 2], buf.at[k, 3], (0, 1)),
-            6: (buf.at[k, 6], buf.at[k, 7], (0, 1)),
-            7: (buf.at[k, 4], buf.at[k, 5], (0, 1)),
+            0: (ref.at[:, chunk(k)], buf.at[k, 1], (XS - 1, 0)),
+            1: (ref.at[:, chunk(k)], buf.at[k, 2], (1, 0)),
+            2: (buf.at[k, 2, first], buf.at[k, 3, first], (1, 0)),
+            3: (buf.at[k, 1, second], buf.at[k, 3, second], (XS - 1, 0)),
+            4: (buf.at[k, 0:XS], buf.at[k, XS:2 * XS], (0, 1)),
         }[i]
         return pltpu.make_async_remote_copy(
-            src_ref=src, dst_ref=dst, send_sem=x_send.at[a, k, i], recv_sem=x_recv.at[a, k, i],
+            src_ref=src, dst_ref=dst, send_sem=x_send.at[a, i], recv_sem=x_recv.at[a, k, i],
             device_id=row_device(*peer), device_id_type=MESH,
         )
 
@@ -124,7 +137,7 @@
         if s == 0:
             src, dst = src.at[part_of[d]], dst.at[part_of[d]]
         return pltpu.make_async_remote_copy(
-            src_ref=src, dst_ref=dst, send_sem=rs_send.at[k, d, s], recv_sem=rs_recv.at[k, d, s],
+            src_ref=src, dst_ref=dst, send_sem=rs_send.at[d, s], recv_sem=rs_recv.at[k, d, s],
             device_id=z_device(1 - 2 * d), device_id_type=MESH,
         )
 
@@ -135,58 +148,65 @@
         if s == steps - 1:
             ref = ref.at[part_of[d]]
         return pltpu.make_async_remote_copy(
-            src_ref=ref, dst_ref=ref, send_sem=ag_send.at[k, d, s], recv_sem=ag_recv.at[k, d, s],
+            src_ref=ref, dst_ref=ref, send_sem=ag_send.at[d, s], recv_sem=ag_recv.at[k, d, s],
             device_id=z_device(1 - 2 * d), device_id_type=MESH,
         )
 
     def store(k, i):
         src, dst = ((wv, nw_ref), (m1v, nm1_ref), (m2v, nm2_ref))[i]
-        return pltpu.make_async_copy(src.at[:, chunk(k)], dst.at[:, chunk(k)], stores.at[i, k])
+        return pltpu.make_async_copy(src.at[:, chunk(k)], dst.at[:, chunk(k)], stores.at[i])
 
     own_c.start()
     load_w.start()
     load_m1.start()
     load_m2.start()
-    pl.semaphore_wait(barrier, 7 + 2 + 8 - jnp.where(at_home, 1, 0))
-    for j in (2, 1, 3, 0):
+    pl.semaphore_wait(barrier, 7 + 4 + 8 - jnp.where(at_home, 1, 0))
+    for i in (3, 1, 2, 0):
         for dc in (0, 1):
-            if j or dc:
-                c_copy(j, dc).start()
+            if i or dc:
+                c_copy(i, dc).start()
     acc[...] = jnp.zeros_like(acc)
 
+    def c_second(k):
+        @pl.when(k == 0)
+        def _():
+            for i in (1, 2, 3):
+                for dc in (0, 1):
+                    c_copy(i, dc).wait_recv()
+            y_copy(0).start()
+            y_copy(1).start()
+
     def x_first(a, k):
+        x_copy(a, k, 0).start()
+        x_copy(a, k, 1).start()
         x_own_copy(a, k).start()
-        for i in (1, 2, 0):
-            x_copy(a, k, i).start()
 
     def x_second(a, k):
+        x_copy(a, k, 1).wait_recv()
+        x_copy(a, k, 2).start()
+        x_copy(a, k, 0).wait_recv()
+        x_copy(a, k, 3).start()
+
+    def x_third(a, k):
+        x_own_copy(a, k).wait()
         x_copy(a, k, 2).wait_recv()
-        x_copy(a, k, 3).start()
-        x_copy(a, k, 1).wait_recv()
+        x_copy(a, k, 3).wait_recv()
         x_copy(a, k, 4).start()
-        x_copy(a, k, 5).start()
-        x_copy(a, k, 6).start()
-
-    def x_third(a, k):
-        x_copy(a, k, 3).wait_recv()
+
+    def x_done(a, k):
         x_copy(a, k, 4).wait_recv()
-        x_copy(a, k, 7).start()
-
-    def x_done(a, k):
-        x_own_copy(a, k).wait()
-        for i in (0, 5, 6, 7):
-            x_copy(a, k, i).wait_recv()
 
     def multiply(k):
         @pl.when(k == 0)
         def _():
             own_c.wait()
-            for j in range(XS):
+            c_copy(0, 1).wait_recv()
+            y_copy(0, arriving=True).wait_recv()
+            y_copy(1, arriving=True).wait_recv()
+            for i in range(XS):
                 for dc in range(2):
-                    if j or dc:
-                        c_copy(j, dc).wait_recv()
-            for slot in range(2 * XS):
-                ct[:, slot * tok:(slot + 1) * tok] = cbuf[slot].T
+                    place = (dc * XS + i) * tok
+                    ct[:, place:place + tok] = cbuf[2 * i + dc].T
 
         x_done(0, k)
         block = hbuf[k].reshape(2 * XS * tok, cut)
@@ -258,55 +278,64 @@
         for d in range(2):
             ag_copy(k, d, steps - 1, arriving=True).wait_recv()
         x_done(1, k)
-        copy = wall[k].reshape(feats, cut)
-        for i in range(XS):
-            block = xbuf[k, 2 * i:2 * i + 2].reshape(2 * tok, cut)
-            acc[2 * i * tok:2 * (i + 1) * tok, :] += lax.dot_general(
-                block, copy, (((1,), (1,)), ((), ())), preferred_element_type=jnp.float32
-            )
-
-    at_mul = 3 * lag_x
-    at_adam = at_mul + steps * lag_z
-    at_out = max(at_adam + steps * lag_z, next_at + 3 * lag_x)
-    plan = []
-    for s in range(steps - 1, 0, -1):
-        plan.append((at_adam + s * lag_z, functools.partial(ag_step, s=s)))
-    for s in range(steps - 1, 0, -1):
-        plan.append((at_mul + s * lag_z, functools.partial(rs_step, s=s)))
-    plan.append((at_adam, adam))
-    for a, base in ((0, 0), (1, next_at)):
-        plan.append((base + 2 * lag_x, functools.partial(x_third, a)))
-        plan.append((base + lag_x, functools.partial(x_second, a)))
-        plan.append((base, functools.partial(x_first, a)))
-    plan.append((at_mul, multiply))
-    plan.append((at_out, forward))
+
+        pair = 2 - n % 2
+
+        @pl.when(lax.rem(k, pair) == pair - 1)
+        def _():
+            copies = [wall[k - j].reshape(feats, cut) for j in range(pair)]
+            for i in range(XS):
+                mine = [xbuf[k - j, 2 * i:2 * i + 2].reshape(2 * tok, cut) for j in range(pair)]
+                acc[2 * i * tok:2 * (i + 1) * tok, :] += sum(
+                    lax.dot_general(a, b, (((1,), (1,)), ((), ())), preferred_element_type=jnp.float32)
+                    for a, b in zip(mine, copies)
+                )
+
+    stages = {
+        "C": c_second,
+        "X1": functools.partial(x_first, 0),
+        "X2": functools.partial(x_second, 0),
+        "X3": functools.partial(x_third, 0),
+        "Y1": functools.partial(x_first, 1),
+        "Y2": functools.partial(x_second, 1),
+        "Y3": functools.partial(x_third, 1),
+        "M": multiply,
+        "A": adam,
+        "O": forward,
+    }
+    for s in range(1, steps):
+        stages[f"R{s}"] = functools.partial(rs_step, s=s)
+        stages[f"G{s}"] = functools.partial(ag_step, s=s)
 
     def tick(t, carry):
-        for start, stage in plan:
+        for name, start in zip(order, delay):
+            if name not in stages:
+                continue
             k = t - start
 
             @pl.when((k >= 0) & (k < n))
-            def _(k=k, stage=stage):
+            def _(k=k, stage=stages[name]):
                 stage(k)
 
         return carry
 
-    lax.fori_loop(0, at_out + n, tick, 0)
-
-    def o_copy(j, dc):
-        px, pc = row_peer(j, dc)
-        return pltpu.make_async_remote_copy(
-            src_ref=part.at[2 * j + dc], dst_ref=got.at[ten * 2 + x_lo], send_sem=o_send.at[2 * j + dc],
+    lax.fori_loop(0, max(delay) + n, tick, 0)
+
+    def o_copy(i, dc):
+        px, pc = row_peer(SIDE[i], dc)
+        slot = XS * dc + i
+        return pltpu.make_async_remote_copy(
+            src_ref=part.at[slot], dst_ref=got.at[ten * 2 + x_lo], send_sem=o_send.at[slot],
             recv_sem=o_recv.at[ten * 2 + x_lo], device_id=at(px, z, pc, node), device_id_type=MESH,
         )
 
     stay = pltpu.make_async_copy(part.at[0], got.at[ten * 2 + x_lo], o_recv.at[ten * 2 + x_lo])
-    for j in (2, 1, 3, 0):
+    for i in (3, 1, 2, 0):
         for dc in range(2):
-            slot = 2 * j + dc
+            slot = XS * dc + i
             part[slot] = (acc[slot * tok:(slot + 1) * tok, :] * factor).astype(jnp.bfloat16)
             if slot:
-                o_copy(j, dc).start()
+                o_copy(i, dc).start()
             else:
 
                 @pl.when(at_home)
@@ -317,24 +346,30 @@
                 def _():
                     o_copy(0, 0).start()
 
-    for j in range(XS):
+    for i in range(XS):
         for dc in range(2):
-            if j or dc:
-                c_copy(j, dc).wait_send()
-
-    def drain(k, carry):
-        for a in range(2):
-            for i in range(8):
-                x_copy(a, k, i).wait_send()
-        for d in range(2):
-            for s in range(steps):
-                rs_copy(k, d, s).wait_send()
-                ag_copy(k, d, s).wait_send()
-        for i in range(3):
-            store(k, i).wait()
-        return carry
-
-    lax.fori_loop(0, n, drain, 0)
+            if i or dc:
+                c_copy(i, dc).wait_send()
+    for d in range(2):
+        y_copy(d).wait_send()
+
+    def all_sent(ref, sem):
+        pltpu.make_async_copy(ref, ref, sem).wait()
+
+    for a, buf in ((0, hbuf), (1, xbuf)):
+        for i in range(2):
+            all_sent(buf.at[:, 0], x_send.at[a, i])
+        for i in range(2, 4):
+            all_sent(buf.at[:, 0, pl.ds(0, half)], x_send.at[a, i])
+        all_sent(buf.at[:, 0:XS], x_send.at[a, 4])
+    for d in range(2):
+        for s in range(steps):
+            sent = send_p.at[:, s, part_of[0]] if s == 0 else send_p.at[:, s]
+            all_sent(sent, rs_send.at[d, s])
+            sent = send_p.at[:, 0, part_of[0]] if s == steps - 1 else send_p.at[:, 0]
+            all_sent(sent, ag_send.at[d, s])
+    for i, (src, dst) in enumerate(((wv, nw_ref), (m1v, nm1_ref), (m2v, nm2_ref))):
+        pltpu.make_async_copy(src, dst, stores.at[i]).wait()
 
     for lo in range(2):
         total = jnp.zeros((tok, feats), jnp.float32)
@@ -345,16 +380,33 @@
         fin[:, lo * feats:(lo + 1) * feats] = total.astype(jnp.bfloat16)
     out = pltpu.make_async_copy(fin, ffn_ref, last)
     out.start()
-    for j in range(XS):
+    for i in range(XS):
         for dc in range(2):
-            if j or dc:
-                o_copy(j, dc).wait_send()
+            if i or dc:
+                o_copy(i, dc).wait_send()
 
     @pl.when(jnp.logical_not(at_home))
     def _():
         o_copy(0, 0).wait_send()
 
     out.wait()
+
+
+def hand_on(*refs):
+    taken, given, held, (ins, outs) = refs[:4], refs[4:8], refs[8:12], refs[12:]
+    moves = []
+    for i in range(4):
+        moves.append((
+            pltpu.make_async_copy(taken[i], held[i], ins.at[i]),
+            pltpu.make_async_copy(held[i], given[i], outs.at[i]),
+        ))
+    for read, _ in moves:
+        read.start()
+    for read, write in moves:
+        read.wait()
+        write.start()
+    for _, write in moves:
+        write.wait()
 
 
 def on_device(prev_hidden, prev_cot, next_hidden, weight, moment1, moment2):
@@ -368,8 +420,8 @@
     bf16, f32 = jnp.bfloat16, jnp.float32
     dma = pltpu.SemaphoreType.DMA
     anywhere = pl.BlockSpec(memory_space=pl.ANY)
-    return pl.pallas_call(
-        functools.partial(kernel, zs, cut, LAG_X, LAG_Z, NEXT_AT),
+    outs = pl.pallas_call(
+        functools.partial(kernel, zs, cut, ORDER, DELAY),
         out_shape=(
             jax.ShapeDtypeStruct((tok, features // 4), bf16),
             jax.ShapeDtypeStruct(weight.shape, f32),
@@ -396,26 +448,36 @@
             pltpu.VMEM((2 * XS, tok, feats), bf16),
             pltpu.VMEM((2 * XS, tok, feats), bf16),
             pltpu.VMEM((tok, 2 * feats), bf16),
-            dma((2, n, 8)),
-            dma((2, n, 8)),
+            dma((2, 5)),
+            dma((2, n, 5)),
             dma((2, n)),
             dma((2 * XS,)),
             dma((2 * XS,)),
             dma(()),
+            dma((2,)),
+            dma((2,)),
+            dma((2, steps)),
             dma((n, 2, steps)),
-            dma((n, 2, steps)),
-            dma((n, 2, steps)),
+            dma((2, steps)),
             dma((n, 2, steps)),
             dma((2 * XS,)),
             dma((2 * XS,)),
             dma((3,)),
-            dma((3, n)),
+            dma((3,)),
             dma(()),
         ],
         compiler_params=pltpu.CompilerParams(
             collective_id=0, has_side_effects=True, vmem_limit_bytes=56 * 2**20
         ),
     )(prev_hidden, prev_cot, next_hidden, weight, moment1, moment2)
+    return pl.pallas_call(
+        hand_on,
+        out_shape=tuple(jax.ShapeDtypeStruct(o.shape, o.dtype) for o in outs),
+        in_specs=[anywhere] * 4,
+        out_specs=(anywhere,) * 4,
+        scratch_shapes=[pltpu.VMEM(o.shape, o.dtype) for o in outs] + [dma((4,)), dma((4,))],
+        compiler_params=pltpu.CompilerParams(vmem_limit_bytes=16 * 2**20),
+    )(*outs)
 
 
 def solution(mesh):

time: 158 us -> 132 us (0.84)
  Pallas kernels: 150 us -> 126 us
  local copies, waits for them, and re-layouts: 6.35 us -> 4.48 us
    pallas_call x1 -> x2, Pallas kernels: 150 us -> 126 us  [the longest x1 124 us: on_device(): pl.pallas_call(functools.partial(kernel, zs, cut, ORDER, DELAY), out_shap...]
    unnamed x8, local copies, waits for them, and re-layouts: 6.35 us -> 4.48 us
where the time goes in v2:
time: 132 us
  Pallas kernels  126 us (95%)
  local copies, waits for them, and re-layouts  4.48 us (3%)
    pallas_call x1, Pallas kernels, on_device(): pl.pallas_call(functools.partial(kernel, zs, cut, ORDER, DELAY), out_shap...  124 us
    unnamed x8, local copies, waits for them, and re-layouts  4.48 us

profile of v2, /device:TPU:1, one launch (start us, length us, event | category | flops | bytes accessed | tf_op | source)
XLA Modules:
  0.0 131.6 jit_solution(184576397427921745)
XLA Ops:
  0.6 124.1 %shard_map.93 = (bf16[128,1024]{1,0:T(8,128)(2,1)}, f32[64,3584]{1,0:T(8,128)}, f32[64,3584]{1,0:T(8,128)}, f32[64,3584]{1,0:T(8,128)}) custom-call(bf16[128,3584]{1,0:T(8,128)(2,1)} %hid_ref.1, bf16[128,4096]{1,0:T(8,128)(2,1)} %cot_ref.1, bf16[128,3584]{1,0:T(8,128)(2,1)} %nxt_ref.1, f32[64,3584]{1,0:T(8,128)} %w_ref.1, f32[64,3584]{1,0:T(8,128)} %m1_ref.1, ...), custom_call_target="tpu_custom_call" | custom-call | tf_op jit(solution)/shard_map/pallas_call | solution.py:423
  124.8 0.0 copy-start
  124.8 1.2 copy-done
  125.9 0.0 copy-start.1
  125.9 1.2 copy-done.1
  127.1 0.0 copy-start.2
  127.1 1.2 copy-done.2
  128.3 0.0 copy-start.3
  128.3 0.9 copy-done.3
  129.2 2.4 %shard_map.94 = (bf16[128,1024]{1,0:T(8,128)(2,1)}, f32[64,3584]{1,0:T(8,128)}, f32[64,3584]{1,0:T(8,128)}, f32[64,3584]{1,0:T(8,128)}) custom-call(bf16[128,1024]{1,0:T(8,128)(2,1)S(1)} %copy-done.3, f32[64,3584]{1,0:T(8,128)S(1)} %copy-done, f32[64,3584]{1,0:T(8,128)S(1)} %copy-done.1, f32[64,3584]{1,0:T(8,128)S(1)} %copy-done.2), custom_call_target="tpu_custom_call" | custom-call | tf_op jit(solution)/shard_map/pallas_call | solution.py:473
Async XLA Ops:
  124.8 1.2 copy-start
  125.9 1.2 copy-start.1
  127.1 1.2 copy-start.2
  128.3 0.9 copy-start.3

commit v3 on v2

--- a/solution.py
+++ b/solution.py
@@ -13,8 +13,8 @@
 MESH = pl.DeviceIdType.MESH
 XS = 4
 CUT = 256
-ORDER = ["C", "Y2", "X3", "Y3", "Y1", "X2", "G1", "G3", "R1", "A", "R3", "X1", "M", "O", "G2", "R2"]
-DELAY = [3, 22, 6, 29, 16, 4, 21, 31, 8, 17, 11, 1, 6, 35, 25, 9]
+ORDER = ["R2", "Y3", "Y1", "X1", "G3", "R1", "Y2", "M", "G2", "X3", "C", "A", "O", "G1", "R3", "X2"]
+DELAY = [9, 30, 12, 0, 32, 7, 25, 5, 23, 4, 1, 13, 38, 18, 10, 2]
 SIDE = (0, 1, XS - 1, 2)
 
 
@@ -89,20 +89,21 @@
     there_rows = pl.multiple_of((1 - parity) * half, half)
     own_c = pltpu.make_async_copy(cot_ref.at[:, cot_block(x, core)], cbuf.at[0], c_own)
 
-    def c_copy(i, dc):
+    def c_copy(i, dc, p=0):
         px, pc = row_peer(SIDE[i], dc)
         slot = 2 * (0, 2, 1, 3)[i] + dc
-        part_rows = pl.ds(here_rows, half) if i else pl.ds(0, tok)
+        part_rows = pl.ds(pl.multiple_of(here_rows + p * quarter, quarter), quarter) if i else pl.ds(0, tok)
         return pltpu.make_async_remote_copy(
             src_ref=cot_ref.at[part_rows, cot_block(px, pc)], dst_ref=cbuf.at[slot, part_rows],
-            send_sem=c_send.at[slot], recv_sem=c_recv.at[slot], device_id=at(px, z, pc, ten), device_id_type=MESH,
-        )
-
-    def y_copy(d, arriving=False):
+            send_sem=c_send.at[slot, p], recv_sem=c_recv.at[slot, p], device_id=at(px, z, pc, ten), device_id_type=MESH,
+        )
+
+    def y_copy(d, p, arriving=False):
         first = there_rows if arriving else here_rows
-        ref = cbuf.at[2:2 * XS, pl.ds(pl.multiple_of(first + d * quarter, quarter), quarter)]
+        eighth = quarter // 2
+        ref = cbuf.at[2:2 * XS, pl.ds(pl.multiple_of(first + p * quarter + d * eighth, eighth), eighth)]
         return pltpu.make_async_remote_copy(
-            src_ref=ref, dst_ref=ref, send_sem=y_send.at[d], recv_sem=y_recv.at[d],
+            src_ref=ref, dst_ref=ref, send_sem=y_send.at[d, p], recv_sem=y_recv.at[d, p],
             device_id=y_device(1 - 2 * d), device_id_type=MESH,
         )
 
@@ -161,20 +162,23 @@
     load_m1.start()
     load_m2.start()
     pl.semaphore_wait(barrier, 7 + 4 + 8 - jnp.where(at_home, 1, 0))
-    for i in (3, 1, 2, 0):
-        for dc in (0, 1):
-            if i or dc:
-                c_copy(i, dc).start()
+    for p in range(2):
+        for i in (3, 1, 2):
+            for dc in (0, 1):
+                c_copy(i, dc, p).start()
+    c_copy(0, 1).start()
     acc[...] = jnp.zeros_like(acc)
 
     def c_second(k):
-        @pl.when(k == 0)
-        def _():
-            for i in (1, 2, 3):
-                for dc in (0, 1):
-                    c_copy(i, dc).wait_recv()
-            y_copy(0).start()
-            y_copy(1).start()
+        for p in range(2):
+
+            @pl.when(k == p)
+            def _(p=p):
+                for i in (1, 2, 3):
+                    for dc in (0, 1):
+                        c_copy(i, dc, p).wait_recv()
+                y_copy(0, p).start()
+                y_copy(1, p).start()
 
     def x_first(a, k):
         x_copy(a, k, 0).start()
@@ -201,9 +205,11 @@
         def _():
             own_c.wait()
             c_copy(0, 1).wait_recv()
-            y_copy(0, arriving=True).wait_recv()
-            y_copy(1, arriving=True).wait_recv()
             for i in range(XS):
+                if i == 1:
+                    for p in range(2):
+                        for d in range(2):
+                            y_copy(d, p, arriving=True).wait_recv()
                 for dc in range(2):
                     place = (dc * XS + i) * tok
                     ct[:, place:place + tok] = cbuf[2 * i + dc].T
@@ -346,12 +352,13 @@
                 def _():
                     o_copy(0, 0).start()
 
-    for i in range(XS):
-        for dc in range(2):
-            if i or dc:
-                c_copy(i, dc).wait_send()
-    for d in range(2):
-        y_copy(d).wait_send()
+    c_copy(0, 1).wait_send()
+    for p in range(2):
+        for i in range(1, XS):
+            for dc in range(2):
+                c_copy(i, dc, p).wait_send()
+        for d in range(2):
+            y_copy(d, p).wait_send()
 
     def all_sent(ref, sem):
         pltpu.make_async_copy(ref, ref, sem).wait()
@@ -371,6 +378,10 @@
     for i, (src, dst) in enumerate(((wv, nw_ref), (m1v, nm1_ref), (m2v, nm2_ref))):
         pltpu.make_async_copy(src, dst, stores.at[i]).wait()
 
+    def done(lo):
+        here = pl.ds(lo * feats, feats)
+        return pltpu.make_async_copy(fin.at[:, here], ffn_ref.at[:, here], last.at[lo])
+
     for lo in range(2):
         total = jnp.zeros((tok, feats), jnp.float32)
         for py in range(4):
@@ -378,8 +389,7 @@
             pltpu.make_async_copy(part.at[0], got.at[slot], o_recv.at[slot]).wait()
             total = total + got[slot].astype(jnp.float32)
         fin[:, lo * feats:(lo + 1) * feats] = total.astype(jnp.bfloat16)
-    out = pltpu.make_async_copy(fin, ffn_ref, last)
-    out.start()
+        done(lo).start()
     for i in range(XS):
         for dc in range(2):
             if i or dc:
@@ -389,7 +399,8 @@
     def _():
         o_copy(0, 0).wait_send()
 
-    out.wait()
+    for lo in range(2):
+        done(lo).wait()
 
 
 def hand_on(*refs):
@@ -451,11 +462,11 @@
             dma((2, 5)),
             dma((2, n, 5)),
             dma((2, n)),
-            dma((2 * XS,)),
-            dma((2 * XS,)),
+            dma((2 * XS, 2)),
+            dma((2 * XS, 2)),
             dma(()),
-            dma((2,)),
-            dma((2,)),
+            dma((2, 2)),
+            dma((2, 2)),
             dma((2, steps)),
             dma((n, 2, steps)),
             dma((2, steps)),
@@ -464,7 +475,7 @@
             dma((2 * XS,)),
             dma((3,)),
             dma((3,)),
-            dma(()),
+            dma((2,)),
         ],
         compiler_params=pltpu.CompilerParams(
             collective_id=0, has_side_effects=True, vmem_limit_bytes=56 * 2**20

time: 132 us -> 132 us (level)
  no operation moved by 1% of the time
where the time goes in v3:
time: 132 us
  Pallas kernels  127 us (96%)
  local copies, waits for them, and re-layouts  4.48 us (3%)
    pallas_call x1, Pallas kernels, on_device(): pl.pallas_call(functools.partial(kernel, zs, cut, ORDER, DELAY), out_shap...  124 us
    unnamed x8, local copies, waits for them, and re-layouts  4.48 us

profile of v3, /device:TPU:1, one launch (start us, length us, event | category | flops | bytes accessed | tf_op | source)
XLA Modules:
  0.0 131.9 jit_solution(2078029670546400869)
XLA Ops:
  0.6 124.4 %shard_map.93 = (bf16[128,1024]{1,0:T(8,128)(2,1)}, f32[64,3584]{1,0:T(8,128)}, f32[64,3584]{1,0:T(8,128)}, f32[64,3584]{1,0:T(8,128)}) custom-call(bf16[128,3584]{1,0:T(8,128)(2,1)} %hid_ref.1, bf16[128,4096]{1,0:T(8,128)(2,1)} %cot_ref.1, bf16[128,3584]{1,0:T(8,128)(2,1)} %nxt_ref.1, f32[64,3584]{1,0:T(8,128)} %w_ref.1, f32[64,3584]{1,0:T(8,128)} %m1_ref.1, ...), custom_call_target="tpu_custom_call" | custom-call | tf_op jit(solution)/shard_map/pallas_call | solution.py:434
  125.0 0.0 copy-start
  125.0 1.2 copy-done
  126.2 0.0 copy-start.1
  126.2 1.2 copy-done.1
  127.4 0.0 copy-start.2
  127.4 1.2 copy-done.2
  128.6 0.0 copy-start.3
  128.6 0.9 copy-done.3
  129.5 2.4 %shard_map.94 = (bf16[128,1024]{1,0:T(8,128)(2,1)}, f32[64,3584]{1,0:T(8,128)}, f32[64,3584]{1,0:T(8,128)}, f32[64,3584]{1,0:T(8,128)}) custom-call(bf16[128,1024]{1,0:T(8,128)(2,1)S(1)} %copy-done.3, f32[64,3584]{1,0:T(8,128)S(1)} %copy-done, f32[64,3584]{1,0:T(8,128)S(1)} %copy-done.1, f32[64,3584]{1,0:T(8,128)S(1)} %copy-done.2), custom_call_target="tpu_custom_call" | custom-call | tf_op jit(solution)/shard_map/pallas_call | solution.py:484
Async XLA Ops:
  125.0 1.2 copy-start
  126.2 1.2 copy-start.1
  127.4 1.2 copy-start.2
  128.6 0.9 copy-start.3
